TPU v7x, 32 devices: a whole 2x2x4 slice. The times are simulated.
32 devices in a mesh: dp: 4 (over y, x), row: 2 (over core), col: 4 (over z).
Axes of the slice: x: 2, y: 2, z: 4, core: 2. Of those that a mesh axis runs over, the one named last changes fastest.
Arguments:
- pixels: bfloat16 [4, 64, 384, 256], P('dp', 'row', 'col'), may hold values from -6 to 6
- hidden_pre: bfloat16 [4, 32, 192, 256], P('dp', 'row', 'col'), may hold values from -6 to 6
- upstream: bfloat16 [4, 16, 96, 512], P('dp', 'row', 'col'), may hold values from -6 to 6
- kernel_first: bfloat16 [3, 3, 256, 256], replicated, may hold values from -0.125 to 0.125
- kernel_second: bfloat16 [3, 3, 256, 512], replicated, may hold values from -0.125 to 0.125
Outputs:
- grad_pixels: bfloat16 [4, 64, 384, 256], P('dp', 'row', 'col')
- grad_kernel_first: float32 [2304, 256], P(('row', 'col'))
- grad_kernel_second: float32 [2304, 512], P(('row', 'col'))
All inputs are finite; a program needn't handle non-finite values.
Results may differ from a plain program's by a relative error of at most 0.0049.
Values may be sent and summed in bfloat16 or wider, within the bound.
A program may use at most 64 MiB of HBM per device.

v0:
```python
import math
import jax
import jax.numpy as jnp
from jax import lax
from jax.sharding import PartitionSpec as P


def shifted(value, axis, by):
    peers = lax.axis_size(axis)
    pairs = [(i, i + by) for i in range(peers) if 0 <= i + by < peers]
    return lax.ppermute(value, axis, pairs)


def extend_field(tile_field):
    from_above = shifted(tile_field[-1], "row", 1)
    from_left = shifted(tile_field[:, -1], "col", 1)
    corner = shifted(from_left[-1:], "row", 1)
    top_row = jnp.concatenate([corner, from_above], axis=0)
    lower_rows = jnp.concatenate([from_left[:, None], tile_field], axis=1)
    return jnp.concatenate([top_row[None], lower_rows], axis=0)


def gather_taps(extended, out_rows, out_cols):
    tap_list = []
    for tap_row in range(3):
        for tap_col in range(3):
            tap_list.append(
                extended[tap_row : tap_row + 2 * out_rows : 2, tap_col : tap_col + 2 * out_cols : 2]
            )
    stacked = jnp.concatenate(tap_list, axis=-1)
    return stacked.reshape(out_rows * out_cols, stacked.shape[-1])


def spread_taps(tap_terms):
    row_count = tap_terms.shape[0]
    col_count = tap_terms.shape[1]
    channels = tap_terms.shape[-1]
    even_part = jnp.pad(tap_terms[:, :, 0], ((0, 1), (0, 0), (0, 0), (0, 0))) + jnp.pad(
        tap_terms[:, :, 2], ((1, 0), (0, 0), (0, 0), (0, 0))
    )
    odd_part = jnp.pad(tap_terms[:, :, 1], ((0, 1), (0, 0), (0, 0), (0, 0)))
    merged = jnp.stack([even_part, odd_part], axis=1).reshape(
        2 * row_count + 2, col_count, 3, channels
    )[: 2 * row_count + 1]
    even_part = jnp.pad(merged[:, :, 0], ((0, 0), (0, 1), (0, 0))) + jnp.pad(
        merged[:, :, 2], ((0, 0), (1, 0), (0, 0))
    )
    odd_part = jnp.pad(merged[:, :, 1], ((0, 0), (0, 1), (0, 0)))
    return jnp.stack([even_part, odd_part], axis=2).reshape(
        2 * row_count + 1, 2 * col_count + 2, channels
    )[:, : 2 * col_count + 1]


def settle_edges(padded):
    interior = padded[1:, 1:]
    from_below = shifted(padded[0, 1:], "row", -1)
    from_right = shifted(padded[:, 0], "col", -1)
    corner = shifted(from_right[:1], "row", -1)
    from_below = from_below.at[-1].add(corner[0])
    interior = interior.at[:, -1].add(from_right[1:])
    return interior.at[-1].add(from_below)


def kernel_gradient(patches, gradient, norm_scale):
    slide_sums = lax.psum(
        lax.dot_general(
            patches, gradient, (((0,), (0,)), ((), ())), preferred_element_type=jnp.float32
        )
        * norm_scale,
        "dp",
    )
    return lax.psum_scatter(slide_sums, ("row", "col"), scatter_dimension=0, tiled=True)


def per_device(pixels, hidden_pre, upstream, kernel_first, kernel_second):
    source = pixels[0]
    hidden = hidden_pre[0]
    cotangent_tile = upstream[0]
    rows_two, cols_two, width_two = cotangent_tile.shape
    rows_one, cols_one, width_one = hidden.shape
    width_zero = source.shape[-1]
    devices_all = lax.axis_size("dp") * lax.axis_size("row") * lax.axis_size("col")
    scale_one = 1.0 / math.sqrt(devices_all * rows_one * cols_one)
    scale_two = 1.0 / math.sqrt(devices_all * rows_two * cols_two)
    flat_second = kernel_second.reshape(9 * width_one, width_two)
    flat_first = kernel_first.reshape(9 * width_zero, width_one)
    cotangent = cotangent_tile.reshape(rows_two * cols_two, width_two)
    terms_two = lax.dot_general(
        cotangent, flat_second, (((1,), (1,)), ((), ())), preferred_element_type=jnp.float32
    )
    grad_active = settle_edges(spread_taps(terms_two.reshape(rows_two, cols_two, 3, 3, width_one)))
    active = jnp.maximum(hidden, 0)
    active_patches = gather_taps(extend_field(active), rows_two, cols_two)
    grad_kernel_second = kernel_gradient(active_patches, cotangent, scale_two)
    grad_pre = jnp.where(hidden > 0, grad_active, 0.0).astype(jnp.bfloat16)
    grad_rows = grad_pre.reshape(rows_one * cols_one, width_one)
    terms_one = lax.dot_general(
        grad_rows, flat_first, (((1,), (1,)), ((), ())), preferred_element_type=jnp.float32
    )
    grad_source = settle_edges(
        spread_taps(terms_one.reshape(rows_one, cols_one, 3, 3, width_zero))
    ).astype(jnp.bfloat16)
    source_patches = gather_taps(extend_field(source), rows_one, cols_one)
    grad_kernel_first = kernel_gradient(source_patches, grad_rows, scale_one)
    return (grad_source[None], grad_kernel_first, grad_kernel_second)


def solution(mesh):
    in_specs = (
        P("dp", "row", "col", None),
        P("dp", "row", "col", None),
        P("dp", "row", "col", None),
        P(),
        P(),
    )
    out_specs = (P("dp", "row", "col", None), P(("row", "col"), None), P(("row", "col"), None))
    return jax.shard_map(
        per_device, mesh=mesh, in_specs=in_specs, out_specs=out_specs, check_vma=False
    )
```

profile of v0, /device:TPU:0, one launch (start us, length us, event | category | flops | bytes accessed | tf_op | source)
XLA Modules:
  0.0 331.8 jit_solution(14036254897099947175)
XLA Ops:
  7.2 1.6 copy-done
  8.8 1.8 fusion.1
  11.6 1.6 copy.44
  13.2 1.8 reshape.226
  15.6 1.3 collective-permute-start
  16.9 0.6 slice_bitcast_fusion.13
  17.5 1.3 collective-permute-start.1
  19.5 6.1 %collective-permute-start.6 = (bf16[32,256]{1,0:T(8,128)(2,1)}, bf16[32,256]{1,0:T(8,128)(2,1)}, u32[]{:S(2)}, u32[]{:S(2)}) collective-permute-start(bf16[32,256]{1,0:T(8,128)(2,1)} %bitcast.134), channel_id=1, source_target_pairs={{0,1},{1,2},{2,3},{4,5},{5,6},{6,7},{8,9},{9,10},{10,11},{12,13},{... | collective-permute-start | bytes 49160 | tf_op jit(solution)/shard_map/ppermute | solution.py:11
  26.2 4.0 %collective-permute-start.8 = (bf16[96,256]{1,0:T(8,128)(2,1)}, bf16[96,256]{1,0:T(8,128)(2,1)}, u32[]{:S(2)}, u32[]{:S(2)}) collective-permute-start(bf16[96,256]{1,0:T(8,128)(2,1)} %slice_bitcast_fusion.14), channel_id=1, source_target_pairs={{0,4},{1,5},{2,6},{3,7},{8,12},{9,13},{10,14},{11,15},{16,20},{17,... | collective-permute-start | bytes 147464 | tf_op jit(solution)/shard_map/ppermute | solution.py:11
  30.3 5.1 %slice.315 = bf16[16,48,256]{2,1,0:T(8,128)(2,1)} slice(bf16[32,96,256]{2,1,0:T(8,128)(2,1)S(1)} %bitcast.138), slice={[0:32:2], [0:96:2], [0:256:1]} | slice | bytes 786432 | tf_op jit(solution)/shard_map/slice | solution.py:28
  35.4 0.7 slice.316
  36.1 1.0 slice.318
  37.2 1.0 slice.319
  38.2 0.7 copy.58
  39.6 2.1 pad_maximum_fusion.2
  41.7 9.2 %slice.314 = bf16[16,48,256]{2,1,0:T(8,128)(2,1)} slice(bf16[32,97,256]{2,1,0:T(8,128)(2,1)} %pad_maximum_fusion.2), slice={[0:32:2], [0:96:2], [0:256:1]} | slice | bytes 786432 | tf_op jit(solution)/shard_map/slice | solution.py:28
  50.9 9.1 %slice.317 = bf16[16,48,256]{2,1,0:T(8,128)(2,1)} slice(bf16[32,97,256]{2,1,0:T(8,128)(2,1)} %pad_maximum_fusion.2), slice={[1:32:2], [0:96:2], [0:256:1]} | slice | bytes 786432 | tf_op jit(solution)/shard_map/slice | solution.py:28
  60.0 1.3 slice.361
  61.2 1.8 collective-permute-start.7
  63.1 0.7 fusion.10
  63.8 1.3 slice.345
  65.1 1.3 collective-permute-start.2
  66.5 0.8 maximum_bitcast_fusion
  67.3 3.0 maximum_maximum_fusion
  70.4 7.6 %slice.311 = bf16[16,48,256]{2,1,0:T(8,128)(2,1)S(1)} slice(bf16[33,97,256]{2,1,0:T(8,128)(2,1)} %maximum_maximum_fusion), slice={[0:32:2], [0:96:2], [0:256:1]} | slice | bytes 786432 | tf_op jit(solution)/shard_map/slice | solution.py:28
  78.0 0.8 constant_dynamic-update-slice_fusion.8
  78.8 9.2 %slice.312 = bf16[16,48,256]{2,1,0:T(8,128)(2,1)} slice(bf16[33,97,256]{2,1,0:T(8,128)(2,1)} %maximum_maximum_fusion), slice={[0:32:2], [1:97:2], [0:256:1]} | slice | bytes 786432 | tf_op jit(solution)/shard_map/slice | solution.py:28
  88.0 7.6 %slice.313 = bf16[16,48,256]{2,1,0:T(8,128)(2,1)S(1)} slice(bf16[33,97,256]{2,1,0:T(8,128)(2,1)} %maximum_maximum_fusion), slice={[0:32:2], [2:97:2], [0:256:1]} | slice | bytes 786432 | tf_op jit(solution)/shard_map/slice | solution.py:28
  95.6 0.7 fusion.12
  96.4 1.3 scatter-add.21
  97.7 0.8 fusion.8
  98.5 1.8 constant_dynamic-update-slice_fusion.7
  100.3 0.8 constant_dynamic-update-slice_fusion.6
  101.1 0.8 constant_dynamic-update-slice_fusion.5
  101.9 0.9 constant_dynamic-update-slice_fusion.4
  102.7 0.8 constant_dynamic-update-slice_fusion.3
  103.6 0.8 constant_dynamic-update-slice_fusion.2
  104.4 0.8 constant_dynamic-update-slice_fusion.1
  105.2 0.8 constant_dynamic-update-slice_fusion
  106.0 4.6 %fusion = f32[2304,256]{1,0:T(8,128)} fusion(bf16[16,48,2304]{2,1,0:T(8,128)(2,1)} %constant_dynamic-update-slice_fusion, f32[16,48,256]{2,1,0:T(8,128)S(1)} %fusion.8, bf16[1,16,48,256]{3,2,1,0:T(8,128)(2,1)S(1)} %copy-done.3), kind=kOutput, calls=%fused_computation.3 | convolution fusion | flops 907345920 | bytes 7077888 | tf_op jit(solution)/shard_map/dot_general | solution.py:66
  110.8 3.3 %collective-permute-start.9 = (bf16[16,256]{1,0:T(8,128)(2,1)S(1)}, bf16[16,256]{1,0:T(8,128)(2,1)S(1)}, u32[]{:S(2)}, u32[]{:S(2)}) collective-permute-start(bf16[16,256]{1,0:T(8,128)(2,1)S(1)} %bitcast.150), channel_id=1, source_target_pairs={{0,1},{1,2},{2,3},{4,5},{5,6},{6,7},{8,9},{9,10},{10,11},{12,13},{... | collective-permute-start | bytes 24584 | tf_op jit(solution)/shard_map/ppermute | solution.py:11
  114.2 3.3 collective-permute-start.11
  119.0 1.3 collective-permute-start.10
  122.4 3.0 convolution_multiply_fusion
  125.6 1.0 copy-done.7
  126.7 1.1 fusion.3
  127.8 0.7 slice_bitcast_fusion.2
  131.3 3.4 %copy.53 = f32[33,49,2,256]{3,2,1,0:T(2,128)} copy(f32[33,49,2,256]{3,1,0,2:T(8,128)S(1)} %pad_maximum_fusion.1) | data formatting | bytes 6623232 | tf_op jit(solution)/shard_map/stack | solution.py:49
  134.7 4.0 %reshape.231 = f32[33,98,256]{2,1,0:T(8,128)S(1)} reshape(f32[33,49,2,256]{3,2,1,0:T(2,128)} %copy.53) | data formatting | bytes 6623232 | tf_op jit(solution)/shard_map/reshape | solution.py:49
  138.8 1.3 collective-permute-start.3
  140.1 0.7 slice_bitcast_fusion.12
  140.8 2.1 slice.352
  142.9 1.3 collective-permute-start.4
  144.2 2.7 collective-permute-done.3
  147.6 1.3 collective-permute-start.5
  148.8 18.9 %reduce-scatter.3.cloned.1.call-done = f32[288,256]{1,0:T(8,128)} async-done(((f32[2304,256]{1,0:T(8,128)}), f32[288,256]{1,0:T(8,128)}) %reduce-scatter.3.cloned.1.call-update) | async-done | bytes 294928 | tf_op jit(solution)/shard_map/reduce_scatter | solution.py:72
  167.7 100.3 %reduce-scatter.5.cloned.1.call-done = f32[288,512]{1,0:T(8,128)} async-done(((f32[2304,512]{1,0:T(8,128)}), f32[288,512]{1,0:T(8,128)}) %reduce-scatter.5.cloned.1.call-update) | async-done | bytes 589840 | tf_op jit(solution)/shard_map/reduce_scatter | solution.py:72
  268.1 0.8 fusion.9
  268.9 1.8 scatter-add.25
  270.7 1.7 fusion.7
  272.4 3.3 convert_bitcast_fusion
  275.7 45.9 %all-reduce.15.cloned.1.call-done = (f32[288,256]{1,0:T(8,128)}, f32[288,512]{1,0:T(8,128)}) async-done(((f32[288,256]{1,0:T(8,128)}, f32[288,512]{1,0:T(8,128)}), (f32[288,256]{1,0:T(8,128)}, f32[288,512]{1,0:T(8,128)})) %all-reduce.15.cloned.1.call-update) | async-done | bytes 884752 | tf_op jit(solution)/shard_map/psum | solution.py:65
  321.6 1.7 copy.111
  323.3 1.9 copy.112
  (96 shorter events, 11.0 us)
Async XLA Ops:
  7.2 1.7 copy-start
  7.2 160.6 %reduce-scatter.3.cloned.1.call-start = ((), (), s32[]{:S(2)}) async-start(), calls=%async_computation.2 | async-start | bytes 2654208 | tf_op jit(solution)/shard_map/reduce_scatter | solution.py:72
  11.6 7.2 %copy-start.2 = (bf16[1,32,96,256]{3,2,1,0:T(8,128)(2,1)S(1)}, bf16[1,32,96,256]{3,2,1,0:T(8,128)(2,1)}, u32[]{:S(2)}) copy-start(bf16[1,32,96,256]{3,2,1,0:T(8,128)(2,1)} %param.17) | copy-start | bytes 4718596
  15.6 47.5 %collective-permute-start = (f32[17,256]{1,0:T(8,128)}, f32[17,256]{1,0:T(8,128)}, u32[]{:S(2)}, u32[]{:S(2)}) collective-permute-start(f32[17,256]{1,0:T(8,128)} %bitcast.133), channel_id=1, source_target_pairs={{1,0},{2,1},{3,2},{5,4},{6,5},{7,6},{9,8},{10,9},{11,10},{13,12},{... | collective-permute-start | bytes 52232 | tf_op jit(solution)/shard_map/ppermute | solution.py:11
  17.5 78.1 %collective-permute-start.1 = (f32[48,256]{1,0:T(8,128)}, f32[48,256]{1,0:T(8,128)}, u32[]{:S(2)}, u32[]{:S(2)}) collective-permute-start(f32[48,256]{1,0:T(8,128)} %slice_bitcast_fusion.13), channel_id=1, source_target_pairs={{4,0},{5,1},{6,2},{7,3},{12,8},{13,9},{14,10},{15,11},{20,16},{21,... | collective-permute-start | bytes 147464 | tf_op jit(solution)/shard_map/ppermute | solution.py:11
  19.5 18.7 %collective-permute-start.6 = (bf16[32,256]{1,0:T(8,128)(2,1)}, bf16[32,256]{1,0:T(8,128)(2,1)}, u32[]{:S(2)}, u32[]{:S(2)}) collective-permute-start(bf16[32,256]{1,0:T(8,128)(2,1)} %bitcast.134), channel_id=1, source_target_pairs={{0,1},{1,2},{2,3},{4,5},{5,6},{6,7},{8,9},{9,10},{10,11},{12,13},{... | collective-permute-start | bytes 49160 | tf_op jit(solution)/shard_map/ppermute | solution.py:11
  26.2 40.3 %collective-permute-start.8 = (bf16[96,256]{1,0:T(8,128)(2,1)}, bf16[96,256]{1,0:T(8,128)(2,1)}, u32[]{:S(2)}, u32[]{:S(2)}) collective-permute-start(bf16[96,256]{1,0:T(8,128)(2,1)} %slice_bitcast_fusion.14), channel_id=1, source_target_pairs={{0,4},{1,5},{2,6},{3,7},{8,12},{9,13},{10,14},{11,15},{16,20},{17,... | collective-permute-start | bytes 147464 | tf_op jit(solution)/shard_map/ppermute | solution.py:11
  39.0 0.6 copy-start.8
  61.2 5.3 %collective-permute-start.7 = (bf16[1,256]{1,0:T(2,128)(2,1)}, bf16[1,256]{1,0:T(2,128)(2,1)}, u32[]{:S(2)}, u32[]{:S(2)}) collective-permute-start(bf16[1,256]{1,0:T(2,128)(2,1)} %slice.361), channel_id=1, source_target_pairs={{0,4},{1,5},{2,6},{3,7},{8,12},{9,13},{10,14},{11,15},{16,20},{17,... | collective-permute-start | bytes 1544 | tf_op jit(solution)/shard_map/ppermute | solution.py:11
  65.1 30.5 %collective-permute-start.2 = (f32[1,256]{1,0:T(1,128)}, f32[1,256]{1,0:T(1,128)}, u32[]{:S(2)}, u32[]{:S(2)}) collective-permute-start(f32[1,256]{1,0:T(1,128)} %slice.345), channel_id=1, source_target_pairs={{4,0},{5,1},{6,2},{7,3},{12,8},{13,9},{14,10},{15,11},{20,16},{21,... | collective-permute-start | bytes 3080 | tf_op jit(solution)/shard_map/ppermute | solution.py:11
  70.4 30.7 %copy-start.6 = (bf16[16,48,256]{2,1,0:T(8,128)(2,1)S(1)}, bf16[16,48,256]{2,1,0:T(8,128)(2,1)}, u32[]{:S(2)}) copy-start(bf16[16,48,256]{2,1,0:T(8,128)(2,1)} %slice.314) | copy-start | bytes 1179652
  78.0 23.9 %copy-start.4 = (bf16[16,48,256]{2,1,0:T(8,128)(2,1)S(1)}, bf16[16,48,256]{2,1,0:T(8,128)(2,1)}, u32[]{:S(2)}) copy-start(bf16[16,48,256]{2,1,0:T(8,128)(2,1)} %slice.315) | copy-start | bytes 1179652
  88.0 15.6 %copy-start.5 = (bf16[16,48,256]{2,1,0:T(8,128)(2,1)S(1)}, bf16[16,48,256]{2,1,0:T(8,128)(2,1)}, u32[]{:S(2)}) copy-start(bf16[16,48,256]{2,1,0:T(8,128)(2,1)} %slice.317) | copy-start | bytes 1179652
  101.1 5.0 %copy-start.3 = (bf16[1,16,48,256]{3,2,1,0:T(8,128)(2,1)S(1)}, bf16[1,16,48,256]{3,2,1,0:T(8,128)(2,1)}, u32[]{:S(2)}) copy-start(bf16[1,16,48,256]{3,2,1,0:T(8,128)(2,1)} %param.18) | copy-start | bytes 1179652
  110.7 157.4 %reduce-scatter.5.cloned.1.call-start = ((), (), s32[]{:S(2)}) async-start(), calls=%async_computation.3 | async-start | bytes 5308416 | tf_op jit(solution)/shard_map/reduce_scatter | solution.py:72
  110.8 8.2 %collective-permute-start.9 = (bf16[16,256]{1,0:T(8,128)(2,1)S(1)}, bf16[16,256]{1,0:T(8,128)(2,1)S(1)}, u32[]{:S(2)}, u32[]{:S(2)}) collective-permute-start(bf16[16,256]{1,0:T(8,128)(2,1)S(1)} %bitcast.150), channel_id=1, source_target_pairs={{0,1},{1,2},{2,3},{4,5},{5,6},{6,7},{8,9},{9,10},{10,11},{12,13},{... | collective-permute-start | bytes 24584 | tf_op jit(solution)/shard_map/ppermute | solution.py:11
  114.2 7.0 %collective-permute-start.11 = (bf16[48,256]{1,0:T(8,128)(2,1)S(1)}, bf16[48,256]{1,0:T(8,128)(2,1)S(1)}, u32[]{:S(2)}, u32[]{:S(2)}) collective-permute-start(bf16[48,256]{1,0:T(8,128)(2,1)S(1)} %slice_bitcast_fusion.16), channel_id=1, source_target_pairs={{0,4},{1,5},{2,6},{3,7},{8,12},{9,13},{10,14},{11,15},{16,20},{17,... | collective-permute-start | bytes 73736 | tf_op jit(solution)/shard_map/ppermute | solution.py:11
  118.1 4.3 %copy-start.9 = (bf16[1,8,24,512]{3,2,1,0:T(8,128)(2,1)S(1)}, bf16[1,8,24,512]{3,2,1,0:T(8,128)(2,1)}, u32[]{:S(2)}) copy-start(bf16[1,8,24,512]{3,2,1,0:T(8,128)(2,1)} %param.19) | copy-start | bytes 589828
  119.0 2.1 collective-permute-start.10
  125.4 1.3 copy-start.7
  125.4 196.2 %all-reduce.15.cloned.1.call-start = ((), (), s32[]{:S(2)}) async-start(), calls=%async_computation.4 | async-start | bytes 1769472 | tf_op jit(solution)/shard_map/psum | solution.py:65
  138.8 8.1 %collective-permute-start.3 = (f32[33,256]{1,0:T(8,128)S(1)}, f32[33,256]{1,0:T(8,128)S(1)}, u32[]{:S(2)}, u32[]{:S(2)}) collective-permute-start(f32[33,256]{1,0:T(8,128)S(1)} %bitcast.148), channel_id=1, source_target_pairs={{1,0},{2,1},{3,2},{5,4},{6,5},{7,6},{9,8},{10,9},{11,10},{13,12},{... | collective-permute-start | bytes 101384 | tf_op jit(solution)/shard_map/ppermute | solution.py:11
  142.9 127.8 %collective-permute-start.4 = (f32[96,256]{1,0:T(8,128)}, f32[96,256]{1,0:T(8,128)S(1)}, u32[]{:S(2)}, u32[]{:S(2)}) collective-permute-start(f32[96,256]{1,0:T(8,128)} %slice_bitcast_fusion.12), channel_id=1, source_target_pairs={{4,0},{5,1},{6,2},{7,3},{12,8},{13,9},{14,10},{15,11},{20,16},{21,... | collective-permute-start | bytes 294920 | tf_op jit(solution)/shard_map/ppermute | solution.py:11
  146.9 0.6 copy-start.10
  147.6 123.1 %collective-permute-start.5 = (f32[1,256]{1,0:T(1,128)S(1)}, f32[1,256]{1,0:T(1,128)S(1)}, u32[]{:S(2)}, u32[]{:S(2)}) collective-permute-start(f32[1,256]{1,0:T(1,128)S(1)} %slice.359), channel_id=1, source_target_pairs={{4,0},{5,1},{6,2},{7,3},{12,8},{13,9},{14,10},{15,11},{20,16},{21,... | collective-permute-start | bytes 3080 | tf_op jit(solution)/shard_map/ppermute | solution.py:11
  270.7 54.5 %copy-start.1 = (bf16[3,3,256,512]{3,2,1,0:T(8,128)(2,1)S(1)}, bf16[3,3,256,512]{3,2,1,0:T(8,128)(2,1)}, u32[]{:S(2)}) copy-start(bf16[3,3,256,512]{3,2,1,0:T(8,128)(2,1)} %param.21) | copy-start | bytes 7077892
Sparse Core Ops, SparseCore 0:
  110.8 56.8 reduce-scatter.2
  170.0 97.9 reduce-scatter.4
  271.2 50.3 all-reduce.14
where the time goes:
time: 335 us; the launch traced here: 332 us
  waiting for transfers between devices  168 us (50%)
  local copies, waits for them, and re-layouts  94.8 us (28%)
  starting transfers between devices  27.9 us (8%)
  other arithmetic  16.2 us (5%)
  between operations  14.4 us (4%)
  matrix products  10.6 us (3%)
    reduce_scatter x2, waiting for transfers between devices, kernel_gradient(): lax.psum_scatter(slide_sums, ('row', 'col'), scatter_dimension=0, tiled=T...  119 us
    slice x18, local copies, waits for them, and re-layouts, gather_taps(): extended[tap_row:tap_row + 2 * out_rows:2, tap_col:tap_col + 2 * out_cols:2]  53.5 us
    psum x1, waiting for transfers between devices, kernel_gradient(): lax.psum(lax.dot_general(patches, gradient, (((0,), (0,)), ((), ())), pre...  45.9 us
    ppermute x12, starting transfers between devices, shifted(): return lax.ppermute(value, axis, pairs)  27.6 us
    unnamed x44, local copies, waits for them, and re-layouts  16.4 us
    dot_general x2, matrix products, kernel_gradient(): lax.dot_general(patches, gradient, (((0,), (0,)), ((), ())), preferred_el...  7.61 us
  transfers between devices with their start and end apart: 15, of which 4 were waited for; matrix products, arithmetic and copies ran while one was open for 28% of the time, Pallas kernels for 0%

commit v1 on v0

--- a/solution.py
+++ b/solution.py
@@ -62,13 +62,14 @@
 
 
 def kernel_gradient(patches, gradient, norm_scale):
-    slide_sums = lax.psum(
+    block = (
         lax.dot_general(
             patches, gradient, (((0,), (0,)), ((), ())), preferred_element_type=jnp.float32
         )
-        * norm_scale,
-        "dp",
+        * norm_scale
     )
+    parts = lax.all_gather(block, "dp", axis=0, tiled=False)
+    slide_sums = parts.sum(axis=0)
     return lax.psum_scatter(slide_sums, ("row", "col"), scatter_dimension=0, tiled=True)
 
 

time: 335 us -> 559 us (1.67)
  waiting for transfers between devices: 168 us -> 371 us
  other arithmetic: 16.2 us -> 32 us
  local copies, waits for them, and re-layouts: 94.8 us -> 101 us
    all_gather x0 -> x2, waiting for transfers between devices: none -> 256 us  [kernel_gradient(): parts = lax.all_gather(block, 'dp', axis=0, tiled=False)]
    psum x1 -> x0, waiting for transfers between devices: 45.9 us -> none  [kernel_gradient(): lax.psum(lax.dot_general(patches, gradient, (((0,), (0,)), ((), ())), pre...]
    reduce_sum x0 -> x2, other arithmetic: none -> 17.5 us  [kernel_gradient(): slide_sums = parts.sum(axis=0)]
    slice x18, local copies, waits for them, and re-layouts: 53.5 us -> 61.5 us  [gather_taps(): extended[tap_row:tap_row + 2 * out_rows:2, tap_col:tap_col + 2 * out_cols:2]]
    unnamed x44 -> x42, local copies, waits for them, and re-layouts: 16.4 us -> 9.11 us
  transfers between devices with their start and end apart: 15 -> 16, of which waited for: 4 -> 4; matrix products, arithmetic and copies ran while one was open for 28% -> 23% of each run, Pallas kernels for 0% -> 0%
where the time goes in v1:
time: 559 us; the launch traced here: 556 us
  waiting for transfers between devices  371 us (66%)
  local copies, waits for them, and re-layouts  101 us (18%)
  other arithmetic  32 us (6%)
  starting transfers between devices  27.2 us (5%)
  between operations  14.5 us (3%)
  matrix products  10.7 us (2%)
    all_gather x2, waiting for transfers between devices, kernel_gradient(): parts = lax.all_gather(block, 'dp', axis=0, tiled=False)  256 us
    reduce_scatter x2, waiting for transfers between devices, kernel_gradient(): lax.psum_scatter(slide_sums, ('row', 'col'), scatter_dimension=0, tiled=T...  115 us
    slice x18, local copies, waits for them, and re-layouts, gather_taps(): extended[tap_row:tap_row + 2 * out_rows:2, tap_col:tap_col + 2 * out_cols:2]  61.5 us
    ppermute x12, starting transfers between devices, shifted(): return lax.ppermute(value, axis, pairs)  26.9 us
    reduce_sum x2, other arithmetic, kernel_gradient(): slide_sums = parts.sum(axis=0)  17.5 us
  transfers between devices with their start and end apart: 16, of which 4 were waited for; matrix products, arithmetic and copies ran while one was open for 23% of the time, Pallas kernels for 0%

profile of v1, /device:TPU:0, one launch (start us, length us, event | category | flops | bytes accessed | tf_op | source)
XLA Modules:
  0.0 556.3 jit_solution(5251457582979202067)
XLA Ops:
  7.2 1.1 slice.360
  8.3 4.9 collective-permute-start.6
  13.3 1.4 slice_bitcast_fusion.14
  14.7 2.1 collective-permute-start.8
  16.8 1.8 fusion.1
  19.5 1.6 copy.44
  21.1 1.8 reshape.226
  23.4 1.3 collective-permute-start
  24.7 0.6 slice_bitcast_fusion.13
  25.4 1.3 collective-permute-start.1
  26.7 5.2 slice.319
  31.9 5.2 slice.318
  37.1 5.2 slice.316
  42.3 5.2 slice.315
  48.1 2.1 pad_maximum_fusion.2
  50.2 7.5 %slice.314 = bf16[16,48,256]{2,1,0:T(8,128)(2,1)S(1)} slice(bf16[32,97,256]{2,1,0:T(8,128)(2,1)} %pad_maximum_fusion.2), slice={[0:32:2], [0:96:2], [0:256:1]} | slice | bytes 786432 | tf_op jit(solution)/shard_map/slice | solution.py:28
  57.8 7.5 %slice.317 = bf16[16,48,256]{2,1,0:T(8,128)(2,1)S(1)} slice(bf16[32,97,256]{2,1,0:T(8,128)(2,1)} %pad_maximum_fusion.2), slice={[1:32:2], [0:96:2], [0:256:1]} | slice | bytes 786432 | tf_op jit(solution)/shard_map/slice | solution.py:28
  65.3 0.7 slice.361
  66.0 3.6 collective-permute-start.7
  69.6 0.7 fusion.10
  70.4 0.7 slice.345
  71.1 1.3 collective-permute-start.2
  72.5 0.8 maximum_bitcast_fusion
  73.3 2.2 maximum_maximum_fusion
  75.5 7.5 %slice.311 = bf16[16,48,256]{2,1,0:T(8,128)(2,1)S(1)} slice(bf16[33,97,256]{2,1,0:T(8,128)(2,1)} %maximum_maximum_fusion), slice={[0:32:2], [0:96:2], [0:256:1]} | slice | bytes 786432 | tf_op jit(solution)/shard_map/slice | solution.py:28
  83.1 0.8 constant_dynamic-update-slice_fusion.8
  83.9 7.6 %slice.313 = bf16[16,48,256]{2,1,0:T(8,128)(2,1)S(1)} slice(bf16[33,97,256]{2,1,0:T(8,128)(2,1)} %maximum_maximum_fusion), slice={[0:32:2], [2:97:2], [0:256:1]} | slice | bytes 786432 | tf_op jit(solution)/shard_map/slice | solution.py:28
  91.5 7.5 %slice.312 = bf16[16,48,256]{2,1,0:T(8,128)(2,1)S(1)} slice(bf16[33,97,256]{2,1,0:T(8,128)(2,1)} %maximum_maximum_fusion), slice={[0:32:2], [1:97:2], [0:256:1]} | slice | bytes 786432 | tf_op jit(solution)/shard_map/slice | solution.py:28
  99.1 0.7 fusion.12
  99.9 1.3 scatter-add.21
  101.2 0.8 fusion.8
  102.0 0.8 constant_dynamic-update-slice_fusion.7
  102.8 0.8 constant_dynamic-update-slice_fusion.6
  103.6 0.9 constant_dynamic-update-slice_fusion.5
  104.4 0.8 constant_dynamic-update-slice_fusion.4
  105.3 0.8 constant_dynamic-update-slice_fusion.3
  106.1 0.8 constant_dynamic-update-slice_fusion.2
  107.0 0.8 constant_dynamic-update-slice_fusion.1
  107.8 0.8 constant_dynamic-update-slice_fusion
  108.6 4.5 fusion
  113.3 4.5 collective-permute-start.9
  117.9 2.7 collective-permute-start.11
  122.1 1.3 collective-permute-start.10
  125.5 3.1 convolution_multiply_fusion
  128.7 84.6 %all-gather.5.cloned.1.call-done = f32[9216,256]{1,0:T(8,128)} async-done(((f32[2304,256]{1,0:T(8,128)}), f32[9216,256]{1,0:T(8,128)}) %all-gather.5.cloned.1.call-update) | async-done | bytes 9437200 | tf_op jit(solution)/shard_map/all_gather | solution.py:71
  213.3 6.0 %reduce_sum.18 = f32[2304,256]{1,0:T(8,128)} reduce(f32[4,2304,256]{2,1,0:T(8,128)} %bitcast.147, f32[]{:T(128)} %constant.173.clone.1), dimensions={0}, to_apply=%region_0.1 | reduce | flops 1769472 | bytes 11796484 | tf_op jit(solution)/shard_map/reduce_sum | solution.py:72
  219.6 171.6 %all-gather.7.cloned.1.call-done = f32[9216,512]{1,0:T(8,128)} async-done(((f32[2304,512]{1,0:T(8,128)}), f32[9216,512]{1,0:T(8,128)}) %all-gather.7.cloned.1.call-update) | async-done | bytes 18874384 | tf_op jit(solution)/shard_map/all_gather | solution.py:71
  391.2 11.5 %reduce_sum.19 = f32[2304,512]{1,0:T(8,128)} reduce(f32[4,2304,512]{2,1,0:T(8,128)} %bitcast.139, f32[]{:T(128)} %constant.173.clone.1), dimensions={0}, to_apply=%region_2.3 | reduce | flops 3538944 | bytes 23592964 | tf_op jit(solution)/shard_map/reduce_sum | solution.py:72
  402.7 1.2 copy-done.8
  403.9 1.1 fusion.3
  408.3 3.4 copy.53
  411.7 5.5 reshape.231
  417.2 1.0 slice.354
  418.2 1.3 collective-permute-start.3
  419.5 0.9 slice_bitcast_fusion.12
  420.4 1.0 slice.353
  421.3 4.1 slice.352
  425.4 1.3 collective-permute-start.4
  426.7 1.3 collective-permute-start.5
  428.1 1.8 scatter-add.25
  430.0 1.7 fusion.7
  431.6 3.3 convert_bitcast_fusion
  434.9 14.1 %reduce-scatter.3.cloned.1.call-done = f32[288,256]{1,0:T(8,128)} async-done(((f32[2304,256]{1,0:T(8,128)}), f32[288,256]{1,0:T(8,128)}) %reduce-scatter.3.cloned.1.call-update) | async-done | bytes 294928 | tf_op jit(solution)/shard_map/reduce_scatter | solution.py:73
  449.0 100.7 %reduce-scatter.5.cloned.1.call-done = f32[288,512]{1,0:T(8,128)} async-done(((f32[2304,512]{1,0:T(8,128)}), f32[288,512]{1,0:T(8,128)}) %reduce-scatter.5.cloned.1.call-update) | async-done | bytes 589840 | tf_op jit(solution)/shard_map/reduce_scatter | solution.py:73
  (99 shorter events, 9.4 us)
Async XLA Ops:
  7.2 9.6 %copy-start = (bf16[3,3,256,512]{3,2,1,0:T(8,128)(2,1)S(1)}, bf16[3,3,256,512]{3,2,1,0:T(8,128)(2,1)}, u32[]{:S(2)}) copy-start(bf16[3,3,256,512]{3,2,1,0:T(8,128)(2,1)} %param.21) | copy-start | bytes 7077892
  7.2 206.1 %all-gather.5.cloned.1.call-start = ((), (), s32[]{:S(2)}) async-start(), calls=%async_computation.4 | async-start | bytes 11796480 | tf_op jit(solution)/shard_map/all_gather | solution.py:71
  8.3 39.2 %collective-permute-start.6 = (bf16[32,256]{1,0:T(8,128)(2,1)S(1)}, bf16[32,256]{1,0:T(8,128)(2,1)S(1)}, u32[]{:S(2)}, u32[]{:S(2)}) collective-permute-start(bf16[32,256]{1,0:T(8,128)(2,1)S(1)} %bitcast.154), channel_id=1, source_target_pairs={{0,1},{1,2},{2,3},{4,5},{5,6},{6,7},{8,9},{9,10},{10,11},{12,13},{... | collective-permute-start | bytes 49160 | tf_op jit(solution)/shard_map/ppermute | solution.py:11
  14.7 57.8 %collective-permute-start.8 = (bf16[96,256]{1,0:T(8,128)(2,1)}, bf16[96,256]{1,0:T(8,128)(2,1)}, u32[]{:S(2)}, u32[]{:S(2)}) collective-permute-start(bf16[96,256]{1,0:T(8,128)(2,1)} %slice_bitcast_fusion.14), channel_id=1, source_target_pairs={{0,4},{1,5},{2,6},{3,7},{8,12},{9,13},{10,14},{11,15},{16,20},{17,... | collective-permute-start | bytes 147464 | tf_op jit(solution)/shard_map/ppermute | solution.py:11
  19.5 7.2 %copy-start.2 = (bf16[1,32,96,256]{3,2,1,0:T(8,128)(2,1)S(1)}, bf16[1,32,96,256]{3,2,1,0:T(8,128)(2,1)}, u32[]{:S(2)}) copy-start(bf16[1,32,96,256]{3,2,1,0:T(8,128)(2,1)} %param.17) | copy-start | bytes 4718596
  23.4 46.1 %collective-permute-start = (f32[17,256]{1,0:T(8,128)}, f32[17,256]{1,0:T(8,128)}, u32[]{:S(2)}, u32[]{:S(2)}) collective-permute-start(f32[17,256]{1,0:T(8,128)} %bitcast.135), channel_id=1, source_target_pairs={{1,0},{2,1},{3,2},{5,4},{6,5},{7,6},{9,8},{10,9},{11,10},{13,12},{... | collective-permute-start | bytes 52232 | tf_op jit(solution)/shard_map/ppermute | solution.py:11
  25.4 73.7 %collective-permute-start.1 = (f32[48,256]{1,0:T(8,128)}, f32[48,256]{1,0:T(8,128)}, u32[]{:S(2)}, u32[]{:S(2)}) collective-permute-start(f32[48,256]{1,0:T(8,128)} %slice_bitcast_fusion.13), channel_id=1, source_target_pairs={{4,0},{5,1},{6,2},{7,3},{12,8},{13,9},{14,10},{15,11},{20,16},{21,... | collective-permute-start | bytes 147464 | tf_op jit(solution)/shard_map/ppermute | solution.py:11
  47.5 0.6 copy-start.10
  66.0 6.5 %collective-permute-start.7 = (bf16[1,256]{1,0:T(2,128)(2,1)S(1)}, bf16[1,256]{1,0:T(2,128)(2,1)S(1)}, u32[]{:S(2)}, u32[]{:S(2)}) collective-permute-start(bf16[1,256]{1,0:T(2,128)(2,1)S(1)} %slice.361), channel_id=1, source_target_pairs={{0,4},{1,5},{2,6},{3,7},{8,12},{9,13},{10,14},{11,15},{16,20},{17,... | collective-permute-start | bytes 1544 | tf_op jit(solution)/shard_map/ppermute | solution.py:11
  71.1 28.0 %collective-permute-start.2 = (f32[1,256]{1,0:T(1,128)S(1)}, f32[1,256]{1,0:T(1,128)S(1)}, u32[]{:S(2)}, u32[]{:S(2)}) collective-permute-start(f32[1,256]{1,0:T(1,128)S(1)} %slice.345), channel_id=1, source_target_pairs={{4,0},{5,1},{6,2},{7,3},{12,8},{13,9},{14,10},{15,11},{20,16},{21,... | collective-permute-start | bytes 3080 | tf_op jit(solution)/shard_map/ppermute | solution.py:11
  83.1 21.4 %copy-start.7 = (bf16[16,48,256]{2,1,0:T(8,128)(2,1)S(1)}, bf16[16,48,256]{2,1,0:T(8,128)(2,1)}, u32[]{:S(2)}) copy-start(bf16[16,48,256]{2,1,0:T(8,128)(2,1)} %slice.315) | copy-start | bytes 1179652
  83.9 21.4 %copy-start.6 = (bf16[16,48,256]{2,1,0:T(8,128)(2,1)S(1)}, bf16[16,48,256]{2,1,0:T(8,128)(2,1)}, u32[]{:S(2)}) copy-start(bf16[16,48,256]{2,1,0:T(8,128)(2,1)} %slice.316) | copy-start | bytes 1179652
  99.1 7.9 %copy-start.5 = (bf16[16,48,256]{2,1,0:T(8,128)(2,1)S(1)}, bf16[16,48,256]{2,1,0:T(8,128)(2,1)}, u32[]{:S(2)}) copy-start(bf16[16,48,256]{2,1,0:T(8,128)(2,1)} %slice.318) | copy-start | bytes 1179652
  102.8 5.0 copy-start.4
  103.6 5.0 copy-start.3
  113.1 278.0 %all-gather.7.cloned.1.call-start = ((), (), s32[]{:S(2)}) async-start(), calls=%async_computation.5 | async-start | bytes 23592960 | tf_op jit(solution)/shard_map/all_gather | solution.py:71
  113.3 8.8 %collective-permute-start.9 = (bf16[16,256]{1,0:T(8,128)(2,1)S(1)}, bf16[16,256]{1,0:T(8,128)(2,1)S(1)}, u32[]{:S(2)}, u32[]{:S(2)}) collective-permute-start(bf16[16,256]{1,0:T(8,128)(2,1)S(1)} %bitcast.156), channel_id=1, source_target_pairs={{0,1},{1,2},{2,3},{4,5},{5,6},{6,7},{8,9},{9,10},{10,11},{12,13},{... | collective-permute-start | bytes 24584 | tf_op jit(solution)/shard_map/ppermute | solution.py:11
  117.9 6.4 %collective-permute-start.11 = (bf16[48,256]{1,0:T(8,128)(2,1)S(1)}, bf16[48,256]{1,0:T(8,128)(2,1)S(1)}, u32[]{:S(2)}, u32[]{:S(2)}) collective-permute-start(bf16[48,256]{1,0:T(8,128)(2,1)S(1)} %slice_bitcast_fusion.16), channel_id=1, source_target_pairs={{0,4},{1,5},{2,6},{3,7},{8,12},{9,13},{10,14},{11,15},{16,20},{17,... | collective-permute-start | bytes 73736 | tf_op jit(solution)/shard_map/ppermute | solution.py:11
  121.6 3.9 copy-start.9
  122.1 2.1 collective-permute-start.10
  128.7 320.3 %reduce-scatter.3.cloned.1.call-start = ((), (), s32[]{:S(2)}) async-start(), calls=%async_computation.2 | async-start | bytes 2654208 | tf_op jit(solution)/shard_map/reduce_scatter | solution.py:73
  219.4 330.4 %reduce-scatter.5.cloned.1.call-start = ((), (), s32[]{:S(2)}) async-start(), calls=%async_computation.3 | async-start | bytes 5308416 | tf_op jit(solution)/shard_map/reduce_scatter | solution.py:73
  402.7 1.3 copy-start.8
  418.2 8.6 %collective-permute-start.3 = (f32[33,256]{1,0:T(8,128)S(1)}, f32[33,256]{1,0:T(8,128)S(1)}, u32[]{:S(2)}, u32[]{:S(2)}) collective-permute-start(f32[33,256]{1,0:T(8,128)S(1)} %bitcast.152), channel_id=1, source_target_pairs={{1,0},{2,1},{3,2},{5,4},{6,5},{7,6},{9,8},{10,9},{11,10},{13,12},{... | collective-permute-start | bytes 101384 | tf_op jit(solution)/shard_map/ppermute | solution.py:11
  425.4 4.5 collective-permute-start.4
  426.7 3.2 collective-permute-start.5
  429.9 119.8 %copy-start.1 = (bf16[3,3,256,512]{3,2,1,0:T(8,128)(2,1)S(1)}, bf16[3,3,256,512]{3,2,1,0:T(8,128)(2,1)}, u32[]{:S(2)}) copy-start(bf16[3,3,256,512]{3,2,1,0:T(8,128)(2,1)} %param.21) | copy-start | bytes 7077892
Sparse Core Ops, SparseCore 0:
  113.3 100.0 all-gather.4
  215.2 175.9 all-gather.6
  394.1 54.8 reduce-scatter.2
  451.7 97.9 reduce-scatter.4
